TPU v7x, 128 devices: a whole 4x4x4 slice. The times are simulated.
128 devices in a mesh: dp: 4 (over y), ep: 32 (over x, z, core).
Axes of the slice: x: 4, y: 4, z: 4, core: 2. Of those that a mesh axis runs over, the one named last changes fastest.
Arguments:
- hidden_rows: bfloat16 [1024, 7168], P(('dp', 'ep')), may hold values from -6 to 6
- expert_ids: int32 [1024, 8], P(('dp', 'ep')), may hold values from 0 to 31, all different within a row; in each aligned block of 8 rows (0 to 7, 8 to 15, ...) at most 3 rows name the same one
- gate_weights: float32 [1024, 8], P(('dp', 'ep')), may hold values from 0.1 to 0.6
- w_gate: bfloat16 [32, 7168, 2048], P('ep', None, 'dp'), may hold values from -0.0625 to 0.0625
- w_up: bfloat16 [32, 7168, 2048], P('ep', None, 'dp'), may hold values from -0.0625 to 0.0625
- w_down: bfloat16 [32, 2048, 7168], P('ep', 'dp'), may hold values from -0.125 to 0.125
- queries: bfloat16 [1024, 64, 576], P(('dp', 'ep')), may hold values from -300 to 300
- suffix_cache: bfloat16 [1024, 128, 576], P(('dp', 'ep')), may hold values from -6 to 6
- prefix_pages: bfloat16 [128, 256, 576], P(('dp', 'ep')), may hold values from -6 to 6
- tree_sizes: int32 [4, 24], P('dp'), may hold values from 1 to 3, 32 in all within a row
Outputs:
- context: bfloat16 [1024, 64, 512], P(('dp', 'ep'))
- expert_mix: bfloat16 [1024, 7168], P(('dp', 'ep'))
Inputs may be any that keep to these rules, and one draw needn't show every extreme that they name: `expert_ids`: each row names 8 different experts; among the leaves of one device no expert is named more than 3 times, a bound that some block reaches. `tree_sizes`: each row sums to 32; some tree of each row spans exactly 3 devices.
All inputs are finite; a program needn't handle non-finite values.
Results may differ from a plain program's by a relative error of at most 0.015.
Values may be sent and summed in bfloat16 or wider, within the bound.
A program may use at most 128 MiB of HBM per device.

v0:
```python
import functools

import jax
import jax.numpy as jnp
from jax import lax
from jax.experimental import pallas as pl
from jax.experimental.pallas import tpu as pltpu
from jax.sharding import PartitionSpec as P

LATENT = 512
TILE = 128
CHUNK = 256
ROWS = 16
score_scale = 192.0 ** (-0.5)
MESH = pl.DeviceIdType.MESH
LINES = (0, 1, -1, 2)
ORDERS = ((1, 2, 0), (2, 0, 1), (0, 1, 2))


class Links:
    def __init__(self, send, recv):
        self.send, self.recv = send, recv
        self.sent, self.got = {}, {}

    def start(self, sent, got, src, dst, device):
        pltpu.make_async_remote_copy(
            src_ref=src,
            dst_ref=dst,
            send_sem=self.send.at[self.sent.setdefault(sent, len(self.sent))],
            recv_sem=self.recv.at[self.got.setdefault(got, len(self.got))],
            device_id=device,
            device_id_type=MESH,
        ).start()

    def recv_wait(self, got, ref):
        pltpu.make_async_copy(ref, ref, self.recv.at[self.got[got]]).wait()

    def send_wait(self, sent, ref):
        pltpu.make_async_copy(ref, ref, self.send.at[self.sent[sent]]).wait()


def cut(part_tiles):
    first = (part_tiles + 1) // 2
    return ((0, first), (first, part_tiles - first))


def kernel(
    data_parts,
    hidden_hbm,
    ids_hbm,
    gates_hbm,
    tree_hbm,
    wg_hbm,
    wu_hbm,
    wd_hbm,
    queries,
    suffix,
    page,
    context,
    out,
    xs,
    wg,
    wu,
    wd,
    accg,
    accu,
    hid,
    dd,
    r1a,
    r2a,
    r1b,
    r2b,
    rc,
    exsrc,
    exin,
    backsrc,
    exback,
    window,
    q_all,
    near_all,
    hidden_rows,
    expert_ids,
    gate_weights,
    tree_sizes,
    wsem,
    asem,
    send_sem,
    recv_sem,
):
    ffq = wg.shape[2]
    half_cols = wg.shape[1]
    y = lax.axis_index("dp")
    ep = lax.axis_index("ep")
    core = lax.rem(ep, 2)
    x = ep // 8
    z = lax.rem(ep // 2, 4)
    here = (x, y, z)
    other = 1 - core

    def shift(axis, by):
        return lax.rem(here[axis] + (by + 4) % 4, 4)

    def device(axis, by):
        place = [x, y, z]
        place[axis] = shift(axis, by)
        return (place[1], place[0] * 8 + place[2] * 2 + core)

    sibling = (y, x * 8 + z * 2 + other)
    ahead = (y, lax.rem(ep + 2, 32))
    behind = (y, lax.rem(ep + 30, 32))

    barrier = pltpu.get_barrier_semaphore()
    greeted = [device(axis, by) for axis in range(3) for by in (1, -1, 2)] + [sibling, ahead, behind]
    for other_device in greeted:
        pl.semaphore_signal(barrier, inc=1, device_id=other_device, device_id_type=MESH)

    first_loads = [
        pltpu.make_async_copy(src, dst, asem.at[3 + i])
        for i, (src, dst) in enumerate(
            (
                (hidden_hbm, hidden_rows),
                (ids_hbm, expert_ids),
                (gates_hbm, gate_weights),
                (tree_hbm, tree_sizes),
            )
        )
    ]
    for load in first_loads:
        load.start()
    loads = []
    for half in range(2):
        rows = pl.ds(half * half_cols, half_cols)
        loads.append(pltpu.make_async_copy(wg_hbm.at[0, rows], wg.at[half], wsem.at[half]))
        loads.append(pltpu.make_async_copy(wu_hbm.at[0, rows], wu.at[half], wsem.at[2 + half]))
    for half in range(2):
        cols = pl.ds(half * half_cols, half_cols)
        loads.append(pltpu.make_async_copy(wd_hbm.at[0, :, cols], wd.at[half], wsem.at[4 + half]))
    att_loads = [
        pltpu.make_async_copy(queries, q_all, asem.at[0]),
        pltpu.make_async_copy(suffix, near_all, asem.at[1]),
        pltpu.make_async_copy(page.at[0], window.at[2], asem.at[2]),
    ]

    for load in first_loads:
        load.wait()
    rows_low = hidden_rows[:, pl.ds(0, half_cols)].astype(jnp.float32)
    rows_high = hidden_rows[:, pl.ds(half_cols, half_cols)].astype(jnp.float32)
    lane = lax.broadcasted_iota(jnp.int32, (8, TILE), 1)
    weight = jnp.zeros((8, TILE), jnp.float32)
    for k in range(expert_ids.shape[1]):
        chosen = lane == expert_ids[:, pl.ds(k, 1)]
        weight = weight + jnp.where(chosen, gate_weights[:, pl.ds(k, 1)], 0.0)
    coarse = weight.astype(jnp.bfloat16).astype(jnp.float32)
    fine = weight - coarse
    exsrc[:, pl.ds(0, half_cols)] = jnp.where(core == 0, rows_high, rows_low)
    exsrc[:, pl.ds(half_cols, TILE)] = jnp.where(core == 0, fine, coarse)

    pl.semaphore_wait(barrier, len(greeted))
    links = Links(send_sem, recv_sem)
    links.start("ex", "ex", exsrc, exin, sibling)
    for load in loads + att_loads:
        load.start()

    starts = []
    spans = []
    for p in range(3):
        starts.append(sum(data_parts[:p]))
        spans.append(data_parts[p] + (1 if p == 2 else 0))

    links.recv_wait("ex", exin)
    theirs = exin[:, pl.ds(0, half_cols)]
    mine = jnp.where(core == 0, rows_low, rows_high)
    low = jnp.where(core == 0, mine, theirs)
    high = jnp.where(core == 0, theirs, mine)
    xs[core, 0, 0, 0, :, pl.ds(0, half_cols)] = jnp.concatenate([low, high], axis=0).astype(jnp.bfloat16)
    theirs = exin[:, pl.ds(half_cols, TILE)]
    mine = jnp.where(core == 0, coarse, fine)
    low = jnp.where(core == 0, mine, theirs)
    high = jnp.where(core == 0, theirs, mine)
    xs[core, 0, 0, 0, :, pl.ds(half_cols, TILE)] = jnp.concatenate([low, high], axis=0).astype(
        jnp.bfloat16
    )

    REST = slice(1, 4)

    def chips(p, moves):
        index = [None, None, None]
        for axis, by in zip(ORDERS[p], moves):
            index[axis] = slice(0, 4) if by is None else by if isinstance(by, slice) else by % 4
        return tuple(index)

    def columns(p, piece):
        return pl.ds((starts[p] + piece[0]) * TILE, piece[1] * TILE)

    def rows_at(p, moves, piece):
        return xs.at[(core,) + chips(p, moves) + (slice(None), columns(p, piece))]

    def whole(p, lead):
        lead = tuple(pl.ds(0, n) if n else 0 for n in lead)
        return xs.at[(0,) + lead + (slice(None), columns(p, (0, spans[p])))]

    def gather(key, m, p, moves, piece, axis, by):
        there = [move - by if a == axis else move for a, move in zip(ORDERS[p], moves)]
        links.start(
            (key, p), (key, p) + m, rows_at(p, moves, piece), rows_at(p, there, piece), device(axis, by)
        )

    def share(name, p, by, line):
        ref = rows_at(p, (None, line, by), (0, spans[p]))
        links.start(("dd", p), ("dd", p, name), ref, ref, sibling)

    DIRS = ((0, 1), (1, -1))

    def start2(p, unit):
        pieces = cut(spans[p])
        for m in range(2):
            for d, by in DIRS:
                gather("a2", (m,), p, (unit, 0, 0), pieces[d ^ m], ORDERS[p][1], by)

    def wait2(p, m):
        links.recv_wait(("a2", p, m), whole(p, (0, 0, 4)))

    def forward2(p):
        wait2(p, 0)
        for d, by in DIRS:
            gather("a2", (2,), p, (None, -by, 0), cut(spans[p])[d], ORDERS[p][1], by)

    def start3(p, line, m, unit=None):
        pieces = cut(spans[p])
        for d, by in DIRS:
            gather("a3", (line, m), p, (unit, line, 0), pieces[d ^ m], ORDERS[p][2], by)

    def wait3(p, line, m):
        links.recv_wait(("a3", p, line, m), whole(p, (0, 0, 4)))

    def forward3(p, line):
        wait3(p, line, 0)
        for d, by in DIRS:
            gather("a3", (line, 2), p, (None, line, -by), cut(spans[p])[d], ORDERS[p][2], by)

    OWN = ((None, 0),)

    def places(p, spots):
        return [chips(p, (None, line, by)) for line, by in spots]

    def stacked(parts):
        parts = [part.reshape(-1, part.shape[-1]) for part in parts]
        return parts[0] if len(parts) == 1 else jnp.concatenate(parts, axis=0)

    def apart(value, ats):
        first = 0
        for at in ats:
            lead = (4,) * sum(isinstance(i, slice) for i in at)
            count = 4 ** len(lead) * ROWS
            yield at, value[first : first + count].reshape(lead + (ROWS, value.shape[-1]))
            first += count

    def layer1(p, spots):
        ats = places(p, spots)
        cols = pl.ds(starts[p] * TILE, data_parts[p] * TILE)
        x0, x1 = [stacked([xs[(half,) + at + (slice(None), cols)] for at in ats]) for half in range(2)]
        for acc, w in ((accg, wg), (accu, wu)):
            got = jnp.dot(x0, w[0, cols, :], preferred_element_type=jnp.float32)
            got = got + jnp.dot(x1, w[1, cols, :], preferred_element_type=jnp.float32)
            for at, rows in apart(got, ats):
                acc[at] += rows

    for p in range(3):
        for by in (1, -1, 2):
            gather("a1", (), p, (0, 0, 0), (0, spans[p]), ORDERS[p][0], by)
    for p in range(3):
        start2(p, 0)
    for p in range(3):
        start3(p, 0, 0, 0)
        start3(p, 0, 1, 0)

    @pl.loop(0, 4)
    def _(i):
        accg[i] = jnp.zeros_like(accg[i])
        accu[i] = jnp.zeros_like(accu[i])

    def beside(line):
        for p in range(3):
            wait3(p, line, 1)
            share(("near", line), p, 1, line)
            share(("near", line), p, -1, line)

    def far(line):
        for p in range(3):
            wait3(p, line, 2)
            share(("far", line in (0, 1)), p, 2, line)

    def first_own(p):
        links.recv_wait(("dd", p, "own"), whole(p, (0, 4, 4)))
        layer1(p, OWN)

    def first_near(p, line):
        links.recv_wait(("dd", p, ("near", line)), whole(p, (0, 2, 4)))
        layer1(p, ((line, 1), (line, -1)))

    def first_far(p, lines):
        links.recv_wait(("dd", p, ("far", 0 in lines)), whole(p, (0, 2, 4)))
        layer1(p, tuple((line, 2) for line in lines))

    for p in range(3):
        links.recv_wait(("a1", p), whole(p, (0, 0, 3)))
        start2(p, REST)
    for p in range(3):
        start3(p, 0, 0, REST)
        start3(p, 0, 1, REST)
        share("own", p, 0, 0)
    for p in range(3):
        forward2(p)
    for p in range(3):
        wait2(p, 1)
        start3(p, 1, 0)
        start3(p, -1, 0)
        share("own", p, 0, 1)
        share("own", p, 0, -1)
    for p in range(3):
        forward3(p, 0)
        start3(p, 1, 1)
    beside(0)
    for p in range(3):
        wait2(p, 2)
        share("own", p, 0, 2)
        start3(p, 2, 0)
        start3(p, -1, 1)
    for load in loads:
        load.wait()
    for p in range(3):
        forward3(p, 1)
        first_own(p)
    for p in range(3):
        forward3(p, -1)
        start3(p, 2, 1)
    far(0)
    first_near(0, 0)
    first_near(1, 0)
    beside(1)
    first_near(2, 0)
    for p in range(3):
        forward3(p, 2)
    beside(-1)
    for p in range(3):
        first_near(p, 1)
    far(1)
    first_near(0, -1)
    first_near(1, -1)
    far(-1)
    first_near(2, -1)
    first_far(0, (0, 1))
    beside(2)
    first_far(1, (0, 1))
    first_far(2, (0, 1))
    first_near(0, 2)
    far(2)
    links.start("page", "page", page.at[0], window.at[0], ahead)
    links.start("page", "page", page.at[0], window.at[4], behind)
    links.start("page", "near", page.at[0], window.at[1 + 2 * core], sibling)
    first_near(1, 2)
    first_near(2, 2)
    for p in range(3):
        first_far(p, (-1, 2))

    @pl.loop(0, 4)
    def _(i):
        @pl.loop(0, 4)
        def _(j):
            tile = pl.ds(half_cols, TILE)
            weight = xs[0, i, j, :, :, tile].astype(jnp.float32) + xs[1, i, j, :, :, tile].astype(
                jnp.float32
            )
            lane = lax.broadcasted_iota(jnp.int32, weight.shape, 2)
            weight = jnp.sum(jnp.where(lane == ep, weight, 0.0), axis=2, keepdims=True)
            gate = accg[i, j]
            hidden = gate * (1.0 / (1.0 + jnp.exp(-gate))) * accu[i, j] * weight
            hid[i, j] = hidden.astype(jnp.bfloat16)

    for p in range(3):
        links.send_wait(("a1", p), whole(p, (0, 0, 3)))
        links.send_wait(("a2", p), whole(p, (0, 3, 4)))
        links.send_wait(("a3", p), whole(p, (3, 4, 4)))
        links.send_wait(("dd", p), whole(p, (4, 4, 4)))

    def layer2(p, spots, half, extra=None):
        ats = places(p, spots)
        cols = pl.ds(starts[p] * TILE, data_parts[p] * TILE)
        rows = stacked([hid[at] for at in ats])
        got = jnp.dot(rows, wd[half, :, cols], preferred_element_type=jnp.float32)
        for at, part in apart(got, ats):
            if extra is not None:
                part = part + extra[at + (slice(None), cols)].astype(jnp.float32)
            xs[(half,) + at + (slice(None), cols)] = part.astype(jnp.bfloat16)

    def add_in(p, moves, piece, sources):
        at = chips(p, moves)
        free = [a for a in range(3) if isinstance(at[a], slice)]
        cols = columns(p, piece)
        width = piece[1] * TILE

        def one(i):
            unit = tuple(i if a in free else at[a] for a in range(3))
            index = (core,) + unit + (slice(None), cols)
            total = xs[index].astype(jnp.float32)
            for ref, lead, first in sources:
                lead = tuple(i if isinstance(l, slice) else l for l in lead)
                total = total + ref[lead + (slice(None), pl.ds(first, width))].astype(jnp.float32)
            xs[index] = total.astype(jnp.bfloat16)

        if free:
            pl.loop(at[free[0]].start, at[free[0]].stop)(one)
        else:
            one(0)

    def block(p, lead):
        lead = tuple(pl.ds(0, n) if n else 0 for n in lead)
        return dd.at[lead + (slice(None), columns(p, (0, data_parts[p])))]

    def make(p, name, spots):
        layer2(p, spots, other)
        for at in places(p, spots):
            at = at + (slice(None), columns(p, (0, data_parts[p])))
            links.start(("rd", p), ("rd", p, name), xs.at[(other,) + at], dd.at[at], sibling)

    def near_place(p, line, unit=None):
        at = chips(p, (unit, line, 0))
        return tuple(at[a] for a in range(3) if a != ORDERS[p][2])

    def scatter(key, m, p, moves, piece, dst, axis, by):
        links.start((key, p), (key, p) + m, rows_at(p, moves, piece), dst, device(axis, by))

    def far1(p, line):
        for d, by in DIRS:
            piece = cut(data_parts[p])[d]
            dst = r1a.at[
                (d,) + near_place(p, line) + (slice(None), pl.ds(starts[p] // 2 * TILE, piece[1] * TILE))
            ]
            scatter("r1", (line, 0), p, (None, line, 2), piece, dst, ORDERS[p][2], by)

    def near1(p, line, m, unit=None):
        last = "last" if unit == 0 else 1
        for d, by in DIRS:
            piece = cut(data_parts[p])[d if m == 2 else 1 - d]
            dst = r2a.at[(d,) + near_place(p, line, unit) + (slice(None), columns(p, piece))]
            scatter("r1", (line, last), p, (unit, line, by), piece, dst, ORDERS[p][2], by)

    def pass1(p, line, unit=None):
        if unit != 0:
            links.recv_wait(("r1", p, line, 0), block(p, (0, 0, 4)))
        for d, by in DIRS:
            piece = cut(data_parts[p])[d]
            place = (d,) + near_place(p, line, unit)
            add_in(p, (unit, line, by), piece, ((r1a, place, starts[p] // 2 * TILE),))
        near1(p, line, 2, unit)

    def lead_of(unit):
        return (0, 0, 2) if unit == 0 else (0, 2, 3) if unit == REST else (0, 2, 4)

    def end1(p, line, unit=None):
        links.recv_wait(("r1", p, line, "last" if unit == 0 else 1), block(p, lead_of(unit)))
        place = near_place(p, line, unit)
        first = starts[p] * TILE
        add_in(
            p,
            (unit, line, 0),
            (0, data_parts[p]),
            ((r2a, (0,) + place, first), (r2a, (1,) + place, first)),
        )

    def far2(p):
        for d, by in DIRS:
            piece = cut(data_parts[p])[d]
            dst = r1b.at[d, :, :, pl.ds(starts[p] // 2 * TILE, piece[1] * TILE)]
            scatter("r2", (0,), p, (None, 2, 0), piece, dst, ORDERS[p][1], by)

    def near2(p, d, m, unit):
        by = (1, -1)[d]
        piece = cut(data_parts[p])[d if m == 2 else 1 - d]
        dst = r2b.at[d, unit, :, columns(p, piece)]
        scatter("r2", ("last" if unit == 0 else 1,), p, (unit, by, 0), piece, dst, ORDERS[p][1], by)

    def pass2(p):
        links.recv_wait(("r2", p, 0), block(p, (0, 0, 4)))
        for d, by in DIRS:
            piece = cut(data_parts[p])[d]
            add_in(p, (None, by, 0), piece, ((r1b, (d, slice(None)), starts[p] // 2 * TILE),))
            near2(p, d, 2, REST)

    def end2(p, unit):
        links.recv_wait(("r2", p, "last" if unit == 0 else 1), block(p, lead_of(unit)))
        first = starts[p] * TILE
        add_in(
            p,
            (unit, 0, 0),
            (0, data_parts[p]),
            ((r2b, (0, unit), first), (r2b, (1, unit), first)),
        )

    def units(p):
        piece = (0, data_parts[p])
        for i, by in ((2, 2), (0, 1), (1, -1)):
            dst = rc.at[i, :, columns(p, piece)]
            scatter("r3", (), p, (by, 0, 0), piece, dst, ORDERS[p][0], by)

    def end3(p):
        links.recv_wait(("r3", p), block(p, (0, 0, 3)))
        first = starts[p] * TILE
        add_in(p, (0, 0, 0), (0, data_parts[p]), tuple((rc, (i,), first) for i in range(3)))

    BACK = (2, 1, -1, 0)

    def settle(p, name, spots):
        links.recv_wait(("rd", p, name), block(p, (0, 4 if name == "own" else len(spots), 4)))
        layer2(p, spots, core, dd)

    def onward(line):
        for p in range(3):
            end1(p, line)
            if line == 2:
                far2(p)
            else:
                near2(p, 0 if line == 1 else 1, 1, REST)

    begin, first_page, span = 0, 0, 0
    for i in range(tree_sizes.shape[1]):
        size = tree_sizes[0, i]
        inside = (begin <= ep) & (ep < begin + size)
        first_page = jnp.where(inside, begin, first_page)
        span = jnp.where(inside, size, span)
        begin = begin + size
    first_slot = jnp.clip(first_page - ep + 2, 0, 2)

    def dot_t(a, b):
        return lax.dot_general(a, b, (((1,), (1,)), ((), ())), preferred_element_type=jnp.float32)

    def attend(i):
        leaves = (2 * i, 2 * i + 1)
        rows = q_all[pl.ds(2 * i, 2)].reshape(2 * q_all.shape[1], q_all.shape[2])
        scores = []
        for k in range(3):
            got = jnp.dot(rows, window[first_slot + k], preferred_element_type=jnp.float32) * score_scale
            scores.append(jnp.where(k < span, got, -1e30))
        near = [
            jnp.dot(q_all[leaf], near_all[leaf], preferred_element_type=jnp.float32) * score_scale
            for leaf in leaves
        ]
        scores.append(jnp.concatenate(near, axis=0))
        top = scores[3].max(axis=1, keepdims=True)
        for k in range(3):
            top = jnp.maximum(top, scores[k].max(axis=1, keepdims=True))
        weights = [jnp.exp(got - top) for got in scores]
        total = weights[3].sum(axis=1, keepdims=True)
        for k in range(3):
            total = total + weights[k].sum(axis=1, keepdims=True)
        probs = [got.astype(jnp.bfloat16) for got in weights]
        heads = q_all.shape[1]
        mixed = jnp.concatenate(
            [
                dot_t(probs[3][n * heads : (n + 1) * heads], near_all[leaf, pl.ds(0, LATENT)])
                for n, leaf in enumerate(leaves)
            ],
            axis=0,
        )
        for k in range(3):
            mixed = mixed + dot_t(probs[k], window[first_slot + k, pl.ds(0, LATENT)])
        context[pl.ds(2 * i, 2)] = (mixed / total).astype(jnp.bfloat16).reshape(2, heads, LATENT)

    FAR, NEAR = ((2, 2),), ((2, 1), (2, -1))
    for p in range(3):
        make(p, "far", FAR)
    for p in range(3):
        make(p, "near", NEAR)
        settle(p, "far", FAR)
        far1(p, 2)
    tasks = [(p, line, ((line, 2), (line, 1), (line, -1))) for line in BACK[1:] for p in range(3)]
    tasks += [(p, "own", OWN) for p in range(3)]
    make(*tasks[0])
    settle(0, "near", NEAR)
    near1(0, 2, 1)
    make(*tasks[1])
    for p in (1, 2):
        settle(p, "near", NEAR)
        near1(p, 2, 1)
    for n, (p, line, spots) in enumerate(tasks):
        if n + 2 < len(tasks):
            make(*tasks[n + 2])
        settle(p, line, spots)
        if line != "own":
            far1(p, line)
            near1(p, line, 1, REST if line == 0 else None)
        if n == 2:
            for q in range(3):
                pass1(q, 2)
            links.recv_wait("page", window.at[pl.ds(0, 2)])
            links.start("page", "near", window.at[4 * other], window.at[3 - 2 * core], sibling)
        if n == 5:
            for q in range(3):
                pass1(q, 1)
            for load in att_loads:
                load.wait()
            links.recv_wait("near", window.at[pl.ds(0, 2)])
            attend(0)
    for p in range(3):
        pass1(p, -1)
    onward(2)
    attend(1)
    onward(1)
    for p in range(3):
        pass1(p, 0, REST)
    onward(-1)
    attend(2)
    for p in range(3):
        pass2(p)
    for p in range(3):
        near1(p, 0, 1, 0)
        pass1(p, 0, 0)
    for p in range(3):
        for d in range(2):
            near2(p, d, 1, 0)
            near2(p, d, 2, 0)
    attend(3)
    for p in range(3):
        end1(p, 0, REST)
    for p in range(3):
        end2(p, REST)
        units(p)
    for p in range(3):
        end1(p, 0, 0)
        end2(p, 0)
    mine = []
    for p in range(3):
        end3(p)
        cols = columns(p, (0, data_parts[p]))
        total = xs[core, 0, 0, 0, :, cols].astype(jnp.float32)
        low, high = total[:8], total[8:]
        backsrc[:, cols] = jnp.where(core == 0, high, low)
        links.start("back", "back", backsrc.at[:, cols], exback.at[:, cols], sibling)
        mine.append(jnp.where(core == 0, low, high))
    mine = jnp.concatenate(mine, axis=1)
    for p in range(3):
        links.send_wait(("rd", p), block(p, (4, 4, 4)))
        links.send_wait(("r1", p), block(p, (3, 4, 4)))
        links.send_wait(("r2", p), block(p, (0, 3, 4)))
        links.send_wait(("r3", p), block(p, (0, 0, 3)))
    links.send_wait("page", window.at[pl.ds(0, 4)])
    links.send_wait("ex", exsrc)
    links.recv_wait("back", exback)
    theirs = exback[...]
    out[:, pl.ds(0, half_cols)] = jnp.where(core == 0, mine, theirs).astype(jnp.bfloat16)
    out[:, pl.ds(half_cols, half_cols)] = jnp.where(core == 0, theirs, mine).astype(jnp.bfloat16)
    links.send_wait("back", backsrc)


def hand_over(context, mix, context_out, mix_out, sems):
    copies = [
        pltpu.make_async_copy(context, context_out, sems.at[0]),
        pltpu.make_async_copy(mix, mix_out, sems.at[1]),
    ]
    for copy in copies:
        copy.start()
    for copy in copies:
        copy.wait()


def local(
    hidden_rows,
    expert_ids,
    gate_weights,
    w_gate,
    w_up,
    w_down,
    queries,
    suffix_cache,
    prefix_pages,
    tree_sizes,
):
    leaves, width = hidden_rows.shape
    half = width // 2
    ffq = w_gate.shape[2]
    pairs = half // TILE // 2
    data_parts = [2 * ((pairs + 2 - p) // 3) for p in range(3)]
    grid = (4, 4, 4)
    bf16, f32 = jnp.bfloat16, jnp.float32
    first_cut = sum(cut(n)[0][1] for n in data_parts) * TILE
    heads, channels = queries.shape[1:]
    suffix_cache, prefix_pages = jnp.swapaxes(suffix_cache, 1, 2), jnp.swapaxes(prefix_pages, 1, 2)
    shapes = [
        ((2,) + grid + (ROWS, half + TILE), bf16),
        ((2, half, ffq), bf16),
        ((2, half, ffq), bf16),
        ((2, ffq, half), bf16),
        (grid + (ROWS, ffq), f32),
        (grid + (ROWS, ffq), f32),
        (grid + (ROWS, ffq), bf16),
        (grid + (ROWS, half), bf16),
        ((2, 4, 4, ROWS, first_cut), bf16),
        ((2, 4, 4, ROWS, half), bf16),
        ((2, 4, ROWS, first_cut), bf16),
        ((2, 4, ROWS, half), bf16),
        ((3, ROWS, half), bf16),
        ((leaves, half + TILE), f32),
        ((leaves, half + TILE), f32),
        ((leaves, half), f32),
        ((leaves, half), f32),
        ((5,) + prefix_pages.shape[1:], bf16),
        (queries.shape, bf16),
        (suffix_cache.shape, bf16),
        ((leaves, width), bf16),
        (expert_ids.shape, expert_ids.dtype),
        (gate_weights.shape, gate_weights.dtype),
    ]
    scratch = [pltpu.VMEM(shape, kind) for shape, kind in shapes]
    scratch.append(pltpu.SMEM(tree_sizes.shape, tree_sizes.dtype))
    scratch += [pltpu.SemaphoreType.DMA((n,)) for n in (6, 7, 27, 130)]
    vmem, hbm = pl.BlockSpec(memory_space=pltpu.VMEM), pl.BlockSpec(memory_space=pl.ANY)
    results = pl.pallas_call(
        functools.partial(kernel, data_parts),
        out_shape=(pltpu.VMEM((leaves, heads, LATENT), bf16), pltpu.VMEM((leaves, width), bf16)),
        in_specs=[hbm] * 10,
        out_specs=(vmem, vmem),
        scratch_shapes=scratch,
        compiler_params=pltpu.CompilerParams(
            collective_id=0, has_side_effects=True, vmem_limit_bytes=61 * 1024 * 1024
        ),
        name="experts",
    )(
        hidden_rows,
        expert_ids,
        gate_weights,
        tree_sizes,
        w_gate,
        w_up,
        w_down,
        queries,
        suffix_cache,
        prefix_pages,
    )
    return pl.pallas_call(
        hand_over,
        out_shape=tuple(jax.ShapeDtypeStruct(r.shape, r.dtype) for r in results),
        in_specs=[vmem] * 2,
        out_specs=(hbm, hbm),
        scratch_shapes=[pltpu.SemaphoreType.DMA((2,))],
        name="results",
    )(*results)


def solution(mesh):
    return jax.shard_map(
        local,
        mesh=mesh,
        in_specs=(
            P(("dp", "ep"), None),
            P(("dp", "ep"), None),
            P(("dp", "ep"), None),
            P("ep", None, "dp"),
            P("ep", None, "dp"),
            P("ep", "dp", None),
            P(("dp", "ep"), None, None),
            P(("dp", "ep"), None, None),
            P(("dp", "ep"), None, None),
            P("dp", None),
        ),
        out_specs=(P(("dp", "ep"), None, None), P(("dp", "ep"), None)),
        check_vma=False,
    )
```

profile of v0, /device:TPU:1, one launch (start us, length us, event | category | flops | bytes accessed | tf_op | source)
XLA Modules:
  0.0 90.2 jit_solution(12309404053096462039)
XLA Ops:
  0.6 86.1 %experts.1 = (bf16[8,64,512]{2,1,0:T(8,128)(2,1)S(1)}, bf16[8,7168]{1,0:T(8,128)(2,1)S(1)}) custom-call(bf16[8,7168]{1,0:T(8,128)(2,1)} %hidden_hbm.1, s32[8,8]{1,0:T(8,128)} %ids_hbm.1, f32[8,8]{1,0:T(8,128)} %gates_hbm.1, s32[1,24]{1,0:T(1,128)} %tree_hbm.1, bf16[1,7168,512]{2,1,0:T(8,128)(2,1)} %wg_hbm.1, bf16[1,7168,512]{2,1,0:T(8,128)(2,1)} %wu_hbm.1, ...), custom_call_target="tpu_custom_call" | custom-call | tf_op jit(solution)/shard_map/experts/pallas_call | solution.py:717
  86.7 0.0 copy-start
  86.7 0.8 copy-done
  87.5 0.0 copy-start.1
  87.5 0.6 copy-done.1
  88.2 1.9 %results.1 = (bf16[8,64,512]{2,1,0:T(8,128)(2,1)}, bf16[8,7168]{1,0:T(8,128)(2,1)}) custom-call(bf16[8,64,512]{2,1,0:T(8,128)(2,1)} %copy-done, bf16[8,7168]{1,0:T(8,128)(2,1)} %copy-done.1), custom_call_target="tpu_custom_call" | custom-call | tf_op jit(solution)/shard_map/results/pallas_call | solution.py:739
Async XLA Ops:
  86.7 0.8 copy-start
  87.5 0.6 copy-start.1
where the time goes:
time: 90.4 us; the launch traced here: 90.2 us
  Pallas kernels  88 us (97%)
  local copies, waits for them, and re-layouts  1.43 us (2%)
    pallas_call x1, Pallas kernels, local(): pl.pallas_call(functools.partial(kernel, data_parts), out_shape=(pltpu.VM...  86.1 us
    pallas_call x1, Pallas kernels, local(): pl.pallas_call(hand_over, out_shape=tuple((jax.ShapeDtypeStruct(r.shape,...  1.89 us

commit v1 on v0

--- a/solution.py
+++ b/solution.py
@@ -736,6 +736,7 @@
         suffix_cache,
         prefix_pages,
     )
+    results = [pltpu.with_memory_space_constraint(r, pltpu.VMEM) for r in results]
     return pl.pallas_call(
         hand_over,
         out_shape=tuple(jax.ShapeDtypeStruct(r.shape, r.dtype) for r in results),

time: 90.4 us -> 87.9 us (0.972)
  local copies, waits for them, and re-layouts: 1.43 us -> 0 us
  Pallas kernels: 88 us -> 86.9 us
    unnamed x4 -> x0, local copies, waits for them, and re-layouts: 1.43 us -> none
    pallas_call x1, Pallas kernels: 1.89 us -> 0.84 us  [local(): pl.pallas_call(hand_over, out_shape=tuple((jax.ShapeDtypeStruct(r.shape,...]
where the time goes in v1:
time: 87.9 us; the launch traced here: 87.7 us
  Pallas kernels  86.9 us (99%)
    pallas_call x1, Pallas kernels, local(): pl.pallas_call(functools.partial(kernel, data_parts), out_shape=(pltpu.VM...  86.1 us

profile of v1, /device:TPU:1, one launch (start us, length us, event | category | flops | bytes accessed | tf_op | source)
XLA Modules:
  0.0 87.7 jit_solution(10320895062076421990)
XLA Ops:
  0.6 86.1 %experts.1 = (bf16[8,64,512]{2,1,0:T(8,128)(2,1)S(1)}, bf16[8,7168]{1,0:T(8,128)(2,1)S(1)}) custom-call(bf16[8,7168]{1,0:T(8,128)(2,1)} %hidden_hbm.1, s32[8,8]{1,0:T(8,128)} %ids_hbm.1, f32[8,8]{1,0:T(8,128)} %gates_hbm.1, s32[1,24]{1,0:T(1,128)} %tree_hbm.1, bf16[1,7168,512]{2,1,0:T(8,128)(2,1)} %wg_hbm.1, bf16[1,7168,512]{2,1,0:T(8,128)(2,1)} %wu_hbm.1, ...), custom_call_target="tpu_custom_call" | custom-call | tf_op jit(solution)/shard_map/experts/pallas_call | solution.py:717
  86.7 0.8 results.1

commit v2 on v1

--- a/solution.py
+++ b/solution.py
@@ -419,7 +419,8 @@
 
     def make(p, name, spots):
         layer2(p, spots, other)
-        for at in places(p, spots):
+        ats = [chips(p, (None, name, REST))] if len(spots) == 3 else places(p, spots)
+        for at in ats:
             at = at + (slice(None), columns(p, (0, data_parts[p])))
             links.start(("rd", p), ("rd", p, name), xs.at[(other,) + at], dd.at[at], sibling)
 

time: 87.9 us -> 87.8 us (level)
  no operation moved by 1% of the time
where the time goes in v2:
time: 87.8 us; the launch traced here: 87.7 us
  Pallas kernels  86.9 us (99%)
    pallas_call x1, Pallas kernels, local(): pl.pallas_call(functools.partial(kernel, data_parts), out_shape=(pltpu.VM...  86 us

profile of v2, /device:TPU:1, one launch (start us, length us, event | category | flops | bytes accessed | tf_op | source)
XLA Modules:
  0.0 87.7 jit_solution(12156999022960567551)
XLA Ops:
  0.6 86.0 %experts.1 = (bf16[8,64,512]{2,1,0:T(8,128)(2,1)S(1)}, bf16[8,7168]{1,0:T(8,128)(2,1)S(1)}) custom-call(bf16[8,7168]{1,0:T(8,128)(2,1)} %hidden_hbm.1, s32[8,8]{1,0:T(8,128)} %ids_hbm.1, f32[8,8]{1,0:T(8,128)} %gates_hbm.1, s32[1,24]{1,0:T(1,128)} %tree_hbm.1, bf16[1,7168,512]{2,1,0:T(8,128)(2,1)} %wg_hbm.1, bf16[1,7168,512]{2,1,0:T(8,128)(2,1)} %wu_hbm.1, ...), custom_call_target="tpu_custom_call" | custom-call | tf_op jit(solution)/shard_map/experts/pallas_call | solution.py:718
  86.7 0.8 results.1
